TPU v7x, 256 devices: a whole 4x4x8 slice. The times are simulated.
256 devices in a mesh: dp: 8 (over z), expert: 32 (over x, y, core).
Axes of the slice: x: 4, y: 4, z: 8, core: 2. Of those that a mesh axis runs over, the one named last changes fastest.
Arguments:
- policy_states: bfloat16 [32, 8, 512, 1024], P('expert', 'dp'), may hold values from -6 to 6
- row_lengths: int32 [256], P('expert'), may hold values from 1 to 512, 65536 in all
- send_order: int32 [256], P('expert'), may hold values from 0 to 7, as said below
- expert_ids: int32 [8, 32, 512, 6], P('dp', 'expert'), may hold values from 0 to 63, all different within a row; in each aligned block of 512 rows (0 to 511, 512 to 1023, ..., all dimensions but the last counted through in order) at most 54 rows name the same one
- gate_codes: int32 [8, 32, 512, 6], P('dp', 'expert'), may hold values from 1 to 15
- w_gate: bfloat16 [64, 1024, 704], P('expert'), may hold values from -0.1875 to 0.1875
- w_up: bfloat16 [64, 1024, 704], P('expert'), may hold values from -0.1875 to 0.1875
- w_down: bfloat16 [64, 704, 1024], P('expert'), may hold values from -0.625 to 0.625
Outputs:
- judged: bfloat16 [256, 512, 1024], P(('dp', 'expert'))
Inputs may be any that keep to these rules, and one draw needn't show every extreme that they name: `send_order`: each aligned block of 8 entries is a permutation of 0 to 7. `expert_ids`: among the 512 token slots of one device no expert is named by more than 54 slots, and some device's slots reach 54 for some expert. `row_lengths`: the largest length is exactly 512.
All inputs are finite; a program needn't handle non-finite values. No bound on the sum of `row_lengths` on one device may be relied on, other than what follows from the above.
Results may differ from a plain program's by a relative error of at most 0.0057.
Values may be sent and summed in bfloat16 or wider, within the bound.
No kernel may reach another device: no remote copies, remote signals or barrier semaphores. Data moves between devices by JAX's collectives and lax.ppermute only.
A program may use at most 192 MiB of HBM per device.

v0:
```python
import jax
import jax.numpy as jnp
from jax import lax
from jax.sharding import PartitionSpec as P


def slot_places(route_flat, experts, capacity):
    count = route_flat.shape[0]
    block = min(512, count)
    blocks = count // block
    labels = jnp.arange(experts, dtype=jnp.int32)
    route_blocks = route_flat.reshape(blocks, block)

    def one_block(offsets, routes):
        hits = (routes[:, None] == labels[None, :]).astype(jnp.int32)
        ranks = jnp.cumsum(hits, axis=0) - 1 + offsets[None, :]
        rank = jnp.sum(hits * ranks, axis=1)
        return (offsets + jnp.sum(hits, axis=0), rank)

    start = jnp.zeros((experts,), jnp.int32)
    unused, ranks = lax.scan(one_block, start, route_blocks)
    return route_flat * capacity + ranks.reshape(count)


def slot_sources(places, fanout, total_slots, filler):
    owners = jnp.arange(places.shape[0], dtype=jnp.int32) // fanout
    return jnp.full((total_slots,), filler, jnp.int32).at[places].set(owners)


def body(policy_states, row_lengths, send_order, expert_ids, gate_codes, w_gate, w_up, w_down):
    features = policy_states.shape[3]
    maxlen = policy_states.shape[2]
    rows_dev = policy_states.shape[1]
    groups = lax.axis_size("expert")
    shards = lax.axis_size("dp")
    own_index = lax.axis_index("dp")
    held_rows = policy_states.reshape(rows_dev, maxlen, features)
    holder = send_order // rows_dev
    within = send_order % rows_dev
    picked = held_rows[within]
    picked = jnp.where((holder == own_index)[:, None, None], picked, jnp.zeros((), picked.dtype))
    picked = picked.reshape(shards, rows_dev, maxlen, features)
    arrived = lax.all_to_all(picked, "dp", split_axis=0, concat_axis=0, tiled=True)
    relaid = jnp.sum(arrived.astype(jnp.float32), axis=0).astype(jnp.bfloat16)
    picked_len = row_lengths[send_order]
    relaid_len = lax.dynamic_slice_in_dim(picked_len, own_index * rows_dev, rows_dev)
    tok_dev = rows_dev * maxlen
    fanout = expert_ids.shape[-1]
    states = relaid.reshape(tok_dev, features)
    route_rows = expert_ids.reshape(tok_dev, fanout)
    gate_code = gate_codes.reshape(tok_dev, fanout).astype(jnp.float32)
    gate_share = gate_code / jnp.sum(gate_code, axis=1, keepdims=True)
    local_experts = w_gate.shape[0]
    experts = local_experts * groups
    capacity = max(2, tok_dev * fanout * 9 // (experts * 8))
    total_slots = experts * capacity
    route_flat = route_rows.reshape(-1)
    places = slot_places(route_flat, experts, capacity)
    padded = jnp.concatenate([states, jnp.zeros((1, features), states.dtype)], axis=0)
    sources = slot_sources(places, fanout, total_slots, tok_dev)
    outbound = padded[sources].reshape(groups, local_experts, capacity, features)
    inbound = lax.all_to_all(outbound, "expert", split_axis=0, concat_axis=0, tiled=True)
    gate_val = jnp.einsum("sekd,edf->sekf", inbound, w_gate, preferred_element_type=jnp.float32)
    up_val = jnp.einsum("sekd,edf->sekf", inbound, w_up, preferred_element_type=jnp.float32)
    hidden = (jax.nn.silu(gate_val) * up_val).astype(jnp.bfloat16)
    outputs = jnp.einsum(
        "sekf,efd->sekd", hidden, w_down, preferred_element_type=jnp.float32
    ).astype(jnp.bfloat16)
    returned = lax.all_to_all(outputs, "expert", split_axis=0, concat_axis=0, tiled=True).reshape(
        total_slots, features
    )
    place_rows = places.reshape(tok_dev, fanout)
    combined = jnp.zeros((tok_dev, features), jnp.float32)
    for pick in range(fanout):
        fetched = returned[place_rows[:, pick]]
        combined = combined + gate_share[:, pick][:, None] * fetched.astype(jnp.float32)
    position = jnp.arange(maxlen, dtype=jnp.int32)
    is_live = (position[None, :] < relaid_len[:, None]).reshape(tok_dev)
    result = jnp.where(is_live[:, None], combined, jnp.float32(0.0)).astype(jnp.bfloat16)
    return result.reshape(rows_dev, maxlen, features)


def solution(mesh):
    in_specs = (
        P("expert", "dp", None, None),
        P("expert"),
        P("expert"),
        P("dp", "expert", None, None),
        P("dp", "expert", None, None),
        P("expert", None, None),
        P("expert", None, None),
        P("expert", None, None),
    )
    out_specs = P(("dp", "expert"), None, None)
    return jax.shard_map(body, mesh=mesh, in_specs=in_specs, out_specs=out_specs, check_vma=False)
```

profile of v0, /device:TPU:12, one launch (start us, length us, event | category | flops | bytes accessed | tf_op | source)
XLA Modules:
  0.0 564.3 jit_solution(13211913348673208866)
XLA Ops:
  0.0 0.8 broadcast_compare_fusion
  0.8 5.1 broadcast_select_fusion.1
  5.9 8.6 %all-to-all-start = ((bf16[8,1,512,1024]{3,2,1,0:T(8,128)(2,1)}), bf16[8,1,512,1024]{3,2,1,0:T(8,128)(2,1)}, u32[]{:S(2)}, u32[]{:S(2)}) async-start(bf16[8,1,512,1024]{3,2,1,0:T(8,128)(2,1)} %broadcast_select_fusion.1), calls=%async_computation | async-start | bytes 16777216 | tf_op jit(solution)/shard_map/all_to_all | solution.py:43
  14.9 10.9 %while.16 = (s32[]{:T(128)}, s32[64]{0:T(128)S(1)}, s32[6,512]{1,0:T(8,128)S(1)}, s32[6,512]{1,0:T(8,128)S(1)}, s32[]{:T(128)}, /*index=5*/s32[]{:T(128)}) while((s32[]{:T(128)}, s32[64]{0:T(128)S(1)}, s32[6,512]{1,0:T(8,128)S(1)}, s32[6,512]{1,0:T(8,128)S(1)}, s32[]{:T(128)}, /*index=5*/s32[]{:T(128)}) %tuple.49), condition=%wide.region_7.8_spmd.clone.clone, body=%wide.region_2.7_spmd.clone.clone.sunk | while | flops 4489795 | bytes 547944 | solution.py:21
  14.9 1.2 reduce-window.22
  16.2 0.2 slice_reduce_fusion.2
  16.4 0.2 fusion.56
  16.8 1.2 reduce-window.22
  18.0 0.2 slice_reduce_fusion.2
  18.2 0.2 fusion.56
  18.6 1.2 reduce-window.22
  19.8 0.2 slice_reduce_fusion.2
  20.1 0.2 fusion.56
  20.4 1.2 reduce-window.22
  21.6 0.2 slice_reduce_fusion.2
  22.2 1.2 reduce-window.22
  23.4 0.2 slice_reduce_fusion.2
  24.0 1.2 reduce-window.22
  25.2 0.2 slice_reduce_fusion.2
  25.8 0.2 mul.136
  26.1 11.8 %scatter_custom_fusion = s32[3456]{0:T(1024)S(1)} fusion(s32[3072]{0:T(1024)S(1)} %bitcast.122, s32[3072]{0:T(1024)S(1)} %add_select_fusion, s32[]{:T(128)} %constant.89.clone.1), kind=kCustom, calls=%fused_computation.78 | custom fusion | bytes 13828 | tf_op jit(solution)/shard_map/scatter | solution.py:27
  37.9 163.3 %all-to-all-done = bf16[8,1,512,1024]{3,2,1,0:T(8,128)(2,1)} async-done(((bf16[8,1,512,1024]{3,2,1,0:T(8,128)(2,1)}), bf16[8,1,512,1024]{3,2,1,0:T(8,128)(2,1)}, u32[]{:S(2)}, u32[]{:S(2)}) %all-to-all-start) | async-done | bytes 8388640 | tf_op jit(solution)/shard_map/all_to_all | solution.py:43
  201.1 6.7 %reduce_sum.46 = bf16[512,1024]{1,0:T(8,128)(2,1)} reduce(bf16[8,1,512,1024]{3,2,1,0:T(8,128)(2,1)} %all-to-all-done, bf16[]{:T(256)} %constant.88.clone.1), dimensions={0,1}, to_apply=%region_1.2 | reduce | flops 3670016 | bytes 9437186 | tf_op jit(solution)/shard_map/reduce_sum | solution.py:44
  207.8 2.3 concatenate.3
  210.1 17.7 %gather_fusion.1 = bf16[3456,1024]{1,0:T(8,128)(2,1)} fusion(bf16[513,1024]{1,0:T(8,128)(2,1)} %concatenate.3, s32[4096]{0:T(1024)S(1)} %pad_clamp_fusion), kind=kCustom, calls=%fused_computation.1 | custom fusion | bytes 14169600 | tf_op jit(solution)/shard_map/gather | solution.py:61
  227.8 8.9 %reshape.392 = bf16[32,2,54,1024]{3,2,1,0:T(8,128)(2,1)} reshape(bf16[3456,1024]{1,0:T(8,128)(2,1)} %gather_fusion.1) | data formatting | bytes 14155776 | tf_op jit(solution)/shard_map/reshape | solution.py:61
  236.6 13.0 %copy.32 = bf16[32,2,54,1024]{3,1,2,0:T(2,128)(2,1)S(1)} copy(bf16[32,2,54,1024]{3,2,1,0:T(8,128)(2,1)} %reshape.392) | data formatting | bytes 14155776 | tf_op jit(solution)/shard_map/reshape | solution.py:61
  249.6 86.3 %all_to_all.15 = bf16[32,2,54,1024]{3,1,2,0:T(2,128)(2,1)S(1)} all-to-all(bf16[32,2,54,1024]{3,1,2,0:T(2,128)(2,1)S(1)} %copy.32), channel_id=1, replica_groups=mesh['dp'=8,'expert'=32] {'expert'}, dimensions={0} | all-to-all | bytes 14155776 | tf_op jit(solution)/shard_map/all_to_all | solution.py:62
  335.9 2.8 copy-done.3
  338.7 10.2 %fusion.12 = f32[2,32,54,704]{3,2,1,0:T(8,128)} fusion(bf16[32,2,54,1024]{3,1,2,0:T(2,128)(2,1)S(1)} %all_to_all.15, bf16[2,1024,704]{1,2,0:T(8,128)(2,1)S(1)} %copy-done.6), kind=kOutput, calls=%fused_computation.32 | convolution fusion | flops 4982833152 | bytes 19693568 | tf_op jit(solution)/shard_map/sekd,edf->sekf/dot_general | solution.py:64
  348.9 20.5 %convert_bitcast_fusion = bf16[32,2,54,1024]{3,2,0,1:T(8,128)(2,1)} fusion(f32[2,32,54,704]{3,2,1,0:T(8,128)} %fusion.12, bf16[2,704,1024]{2,1,0:T(8,128)(2,1)S(1)} %copy-done, bf16[32,2,54,1024]{3,1,2,0:T(2,128)(2,1)} %copy-done.3, bf16[2,1024,704]{1,2,0:T(8,128)(2,1)} %param.15), kind=kOutput, calls=%fused_computation.31 | convolution fusion | flops 9983803392 | bytes 29655040 | tf_op jit(solution)/shard_map/sekf,efd->sekd/dot_general | solution.py:66
  369.4 14.7 %copy.35 = bf16[32,2,54,1024]{3,1,2,0:T(2,128)(2,1)} copy(bf16[32,2,54,1024]{3,2,0,1:T(8,128)(2,1)} %convert_bitcast_fusion) | data formatting | bytes 14155776 | tf_op jit(solution)/shard_map/convert_element_type | solution.py:68
  384.1 8.2 %all-to-all-start.2 = ((bf16[32,2,54,1024]{3,1,2,0:T(2,128)(2,1)}), bf16[32,2,54,1024]{3,1,2,0:T(2,128)(2,1)}, u32[]{:S(2)}, u32[]{:S(2)}) async-start(bf16[32,2,54,1024]{3,1,2,0:T(2,128)(2,1)} %copy.35), calls=%async_computation.2 | async-start | bytes 14155776 | tf_op jit(solution)/shard_map/all_to_all | solution.py:69
  392.3 0.2 reshape.394
  392.6 0.6 gather_fusion
  393.2 0.6 dynamic_slice.10
  393.8 0.6 iota_compare_fusion.2
  394.5 0.8 fusion.38
  395.5 101.9 %all-to-all-done.2 = bf16[32,2,54,1024]{3,1,2,0:T(2,128)(2,1)} async-done(((bf16[32,2,54,1024]{3,1,2,0:T(2,128)(2,1)}), bf16[32,2,54,1024]{3,1,2,0:T(2,128)(2,1)}, u32[]{:S(2)}, u32[]{:S(2)}) %all-to-all-start.2) | async-done | bytes 7077920 | tf_op jit(solution)/shard_map/all_to_all | solution.py:69
  497.4 8.5 %copy.36 = bf16[32,2,54,1024]{3,2,1,0:T(8,128)(2,1)} copy(bf16[32,2,54,1024]{3,1,2,0:T(2,128)(2,1)} %all-to-all-done.2) | data formatting | bytes 14155776 | tf_op jit(solution)/shard_map/all_to_all | solution.py:69
  505.9 8.9 %reshape.393 = bf16[3456,1024]{1,0:T(8,128)(2,1)} reshape(bf16[32,2,54,1024]{3,2,1,0:T(8,128)(2,1)} %copy.36) | data formatting | bytes 14155776 | tf_op jit(solution)/shard_map/reshape | solution.py:69
  514.7 7.4 %gather_fusion.7 = bf16[512,1024]{1,0:T(8,128)(2,1)} fusion(bf16[3456,1024]{1,0:T(8,128)(2,1)} %reshape.393, s32[1024]{0:T(1024)S(1)} %get-tuple-element.127), kind=kCustom, calls=%fused_computation.7 | custom fusion | bytes 2099200 | tf_op jit(solution)/shard_map/gather | solution.py:75
  522.1 7.4 %gather_fusion.6 = bf16[512,1024]{1,0:T(8,128)(2,1)} fusion(bf16[3456,1024]{1,0:T(8,128)(2,1)} %reshape.393, s32[1024]{0:T(1024)S(1)} %get-tuple-element.128), kind=kCustom, calls=%fused_computation.6 | custom fusion | bytes 2099200 | tf_op jit(solution)/shard_map/gather | solution.py:75
  529.5 7.4 %gather_fusion.5 = bf16[512,1024]{1,0:T(8,128)(2,1)} fusion(bf16[3456,1024]{1,0:T(8,128)(2,1)} %reshape.393, s32[1024]{0:T(1024)S(1)} %get-tuple-element.129), kind=kCustom, calls=%fused_computation.5 | custom fusion | bytes 2099200 | tf_op jit(solution)/shard_map/gather | solution.py:75
  536.9 7.7 %gather_fusion.4 = bf16[512,1024]{1,0:T(8,128)(2,1)} fusion(bf16[3456,1024]{1,0:T(8,128)(2,1)} %reshape.393, s32[1024]{0:T(1024)S(1)} %get-tuple-element.130), kind=kCustom, calls=%fused_computation.4 | custom fusion | bytes 2099200 | tf_op jit(solution)/shard_map/gather | solution.py:75
  544.6 7.4 %gather_fusion.3 = bf16[512,1024]{1,0:T(8,128)(2,1)} fusion(bf16[3456,1024]{1,0:T(8,128)(2,1)} %reshape.393, s32[1024]{0:T(1024)S(1)} %get-tuple-element.131), kind=kCustom, calls=%fused_computation.3 | custom fusion | bytes 2099200 | tf_op jit(solution)/shard_map/gather | solution.py:75
  552.0 7.6 %gather_fusion.2 = bf16[512,1024]{1,0:T(8,128)(2,1)} fusion(bf16[3456,1024]{1,0:T(8,128)(2,1)} %reshape.393, s32[1024]{0:T(1024)S(1)} %get-tuple-element.132), kind=kCustom, calls=%fused_computation.2 | custom fusion | bytes 2099200 | tf_op jit(solution)/shard_map/gather | solution.py:75
  559.5 4.3 fusion.33
  (80 shorter events, 2.0 us)
Async XLA Ops:
  0.0 348.9 %copy-start = (bf16[2,704,1024]{2,1,0:T(8,128)(2,1)S(1)}, bf16[2,704,1024]{2,1,0:T(8,128)(2,1)}, u32[]{:S(2)}) copy-start(bf16[2,704,1024]{2,1,0:T(8,128)(2,1)} %param.17) | copy-start | bytes 8650756
  5.9 8.6 %copy-start.5 = (s32[1,1,512,6]{2,1,3,0:T(1,128)S(1)}, s32[1,1,512,6]{2,1,3,0:T(1,128)}, u32[]{:S(2)}) copy-start(s32[1,1,512,6]{2,1,3,0:T(1,128)} %param.13) | copy-start | bytes 36868
  5.9 195.2 %all-to-all-start = ((bf16[8,1,512,1024]{3,2,1,0:T(8,128)(2,1)}), bf16[8,1,512,1024]{3,2,1,0:T(8,128)(2,1)}, u32[]{:S(2)}, u32[]{:S(2)}) async-start(bf16[8,1,512,1024]{3,2,1,0:T(8,128)(2,1)} %broadcast_select_fusion.1), calls=%async_computation | async-start | bytes 16777216 | tf_op jit(solution)/shard_map/all_to_all | solution.py:43
  249.6 89.1 %copy-start.6 = (bf16[2,1024,704]{1,2,0:T(8,128)(2,1)S(1)}, bf16[2,1024,704]{1,2,0:T(8,128)(2,1)}, u32[]{:S(2)}) copy-start(bf16[2,1024,704]{1,2,0:T(8,128)(2,1)} %param.16) | copy-start | bytes 8650756
  335.9 2.8 copy-start.3
  384.1 8.4 %copy-start.4 = (s32[1,1,512,6]{2,1,3,0:T(1,128)S(1)}, s32[1,1,512,6]{2,1,3,0:T(1,128)}, u32[]{:S(2)}) copy-start(s32[1,1,512,6]{2,1,3,0:T(1,128)} %param.14) | copy-start | bytes 36868
  384.1 8.5 %copy-start.7 = (s32[8]{0:T(128)S(1)}, s32[8]{0:T(128)}, u32[]{:S(2)}) copy-start(s32[8]{0:T(128)} %param.12) | copy-start | bytes 100
  384.1 8.5 %copy-start.2 = (s32[8]{0:T(128)S(1)}, s32[8]{0:T(128)}, u32[]{:S(2)}) copy-start(s32[8]{0:T(128)} %param.11) | copy-start | bytes 100
  384.1 113.3 %all-to-all-start.2 = ((bf16[32,2,54,1024]{3,1,2,0:T(2,128)(2,1)}), bf16[32,2,54,1024]{3,1,2,0:T(2,128)(2,1)}, u32[]{:S(2)}, u32[]{:S(2)}) async-start(bf16[32,2,54,1024]{3,1,2,0:T(2,128)(2,1)} %copy.35), calls=%async_computation.2 | async-start | bytes 14155776 | tf_op jit(solution)/shard_map/all_to_all | solution.py:69
  552.0 11.9 %copy-start.1 = (bf16[2,704,1024]{2,1,0:T(8,128)(2,1)S(1)}, bf16[2,704,1024]{2,1,0:T(8,128)(2,1)}, u32[]{:S(2)}) copy-start(bf16[2,704,1024]{2,1,0:T(8,128)(2,1)} %param.17) | copy-start | bytes 8650756
where the time goes:
time: 572 us; the launch traced here: 564 us
  waiting for transfers between devices  265 us (46%)
  local copies, waits for them, and re-layouts  137 us (24%)
  blocking collectives  86.3 us (15%)
  matrix products  30.7 us (5%)
  other arithmetic  27.3 us (5%)
  starting transfers between devices  16.8 us (3%)
    all_to_all x1, waiting for transfers between devices, body(): lax.all_to_all(picked, 'dp', split_axis=0, concat_axis=0, tiled=True)  163 us
    all_to_all x1, waiting for transfers between devices, body(): lax.all_to_all(outputs, 'expert', split_axis=0, concat_axis=0, tiled=True)  102 us
    all_to_all x1, blocking collectives, body(): lax.all_to_all(outbound, 'expert', split_axis=0, concat_axis=0, tiled=True)  86.3 us
    gather x6, local copies, waits for them, and re-layouts, body(): fetched = returned[place_rows[:, pick]]  44.8 us
    reshape x2, local copies, waits for them, and re-layouts, body(): padded[sources].reshape(groups, local_experts, capacity, features)  21.8 us
    dot_general x1, matrix products, body(): jnp.einsum('sekf,efd->sekd', hidden, w_down, preferred_element_type=jnp.f...  20.5 us
    gather x1, local copies, waits for them, and re-layouts, body(): padded[sources].reshape(groups, local_experts, capacity, features)  17.7 us
    convert_element_type x1, local copies, waits for them, and re-layouts, body(): outputs = jnp.einsum('sekf,efd->sekd', hidden, w_down, preferred_element_...  14.7 us
  transfers between devices with their start and end apart: 2, of which 2 were waited for; matrix products, arithmetic and copies ran while one was open for 5% of the time, Pallas kernels for 0%

commit v1 on v0

v1 whole, which is shorter than its diff:
```python
import functools

import jax
import jax.numpy as jnp
from jax import lax
from jax.experimental import pallas as pl
from jax.experimental.pallas import tpu as pltpu
from jax.sharding import Mesh, PartitionSpec as P

F32 = jnp.float32
BF16 = jnp.bfloat16
I32 = jnp.int32
ALL = ("dp", "x", "y", "core")
PLANE = ("x", "y", "core")
CHUNKS = 2
BLOCK = 256
PICK = 64


def one_hot(rows, columns):
    return (rows[:, None] == columns[None, :]).astype(BF16)


def pick(matrix, values):
    return jnp.dot(matrix, values, preferred_element_type=F32).astype(BF16)


def shift(value, axis, by):
    size = lax.axis_size(axis)
    return lax.ppermute(value, axis, [(i, (i + by) % size) for i in range(size)])


def ring_sum(value, axis):
    rows = value.shape[0] // 4
    half = rows // 2
    own, after, across, before = (value[i * rows : (i + 1) * rows] for i in range(4))
    low = shift(across[:half], axis, -1)
    high = shift(across[half:], axis, 1)
    before = jnp.concatenate(
        [(before[:half].astype(F32) + low.astype(F32)).astype(BF16), before[half:]]
    )
    after = jnp.concatenate(
        [after[:half], (after[half:].astype(F32) + high.astype(F32)).astype(BF16)]
    )
    one = shift(before, axis, -1)
    two = shift(after, axis, 1)
    return (own.astype(F32) + one.astype(F32) + two.astype(F32)).astype(BF16)


def expert_kernel(
    starts, picks, tiles, source, states, ranks, shares,
    gate0, up0, down0, gate1, up1, down1, out_a, out_b, rows_ref,
):
    step = pl.program_id(0)
    blocks = ranks.shape[0]
    half = out_a.shape[1]

    def mask_of(block, part):
        lane_rank = ranks[block]
        wanted = (lax.broadcasted_iota(I32, (PICK, BLOCK), 0) + part * PICK).astype(F32)
        return [jnp.where(lane_rank[e : e + 1, :] == wanted, 1.0, 0.0) for e in range(4)]

    def place(expert, block, part):
        return pl.ds(pl.multiple_of(starts[expert * blocks + block] + part * PICK, 16), PICK)

    @pl.when(step == 0)
    def _():
        def one_block(block, carry):
            held = jnp.concatenate([states[source[2 * block]], states[source[2 * block + 1]]])

            def one_part(part, carry):
                mask = jnp.concatenate(mask_of(block, part)).astype(BF16)
                got = jnp.dot(mask, held, preferred_element_type=F32).astype(BF16)
                for e in range(4):
                    rows_ref[e, place(e, block, part), :] = got[e * PICK : (e + 1) * PICK]
                return carry

            return lax.fori_loop(0, picks[block], one_part, carry)

        lax.fori_loop(0, blocks, one_block, 0)

    def feed_forward(expert, gate, up, down):
        def one_tile(tile, carry):
            at = pl.ds(pl.multiple_of(tile * BLOCK, BLOCK), BLOCK)
            held = rows_ref[expert, at, :]
            gated = jnp.dot(held, gate[0], preferred_element_type=F32)
            raised = jnp.dot(held, up[0], preferred_element_type=F32)
            hidden = (gated / (1.0 + jnp.exp(-gated)) * raised).astype(BF16)
            rows_ref[expert, at, :] = jnp.dot(
                hidden, down[0], preferred_element_type=F32
            ).astype(BF16)
            return carry

        lax.fori_loop(0, tiles[expert], one_tile, 0)

    @pl.when((step == 1) | (step == 2))
    def _():
        feed_forward(step - 1, gate0, up0, down0)

    @pl.when((step == 3) | (step == 4))
    def _():
        feed_forward(step - 1, gate1, up1, down1)

    @pl.when(step == 5)
    def _():
        def one_block(block, carry):
            share = shares[block]

            def one_part(part, total):
                masks = mask_of(block, part)
                weight = jnp.concatenate([masks[e] * share[e : e + 1, :] for e in range(4)])
                high = weight.astype(BF16)
                low = (weight - high.astype(F32)).astype(BF16)
                made = jnp.concatenate([rows_ref[e, place(e, block, part), :] for e in range(4)])
                dims = (((0,), (0,)), ((), ()))
                total = total + lax.dot_general(high, made, dims, preferred_element_type=F32)
                return total + lax.dot_general(low, made, dims, preferred_element_type=F32)

            total = lax.fori_loop(
                0, picks[block], one_part, jnp.zeros((BLOCK, out_a.shape[2]), F32)
            ).astype(BF16)
            for j in range(2):
                at = 2 * block + j
                base = j * 2 * half
                out_a[lax.rem(at, 4) * 4 + lax.div(at, 4)] = total[base : base + half]
                out_b[at] = total[base + half : base + 2 * half]
            return carry

        lax.fori_loop(0, blocks, one_block, 0)


def run_experts(starts, picks, tiles, source, states, ranks, shares, own, other):
    features = states.shape[2]
    hidden = own[0].shape[2]
    blocks = ranks.shape[0]
    slots, tokens = states.shape[0], states.shape[1]
    half = tokens // 2
    whole3 = lambda i, *_: (0, 0, 0)
    first = lambda i, *_: (jnp.clip(i - 1, 0, 1), 0, 0)
    second = lambda i, *_: (jnp.clip(i - 3, 0, 1), 0, 0)
    weights = lambda at: [
        pl.BlockSpec((1, features, hidden), at),
        pl.BlockSpec((1, features, hidden), at),
        pl.BlockSpec((1, hidden, features), at),
    ]
    shape = jax.ShapeDtypeStruct((slots, half, features), BF16)
    return pl.pallas_call(
        expert_kernel,
        grid_spec=pltpu.PrefetchScalarGridSpec(
            num_scalar_prefetch=4,
            grid=(6,),
            in_specs=[
                pl.BlockSpec(states.shape, whole3),
                pl.BlockSpec(ranks.shape, whole3),
                pl.BlockSpec(shares.shape, whole3),
                *weights(first),
                *weights(second),
            ],
            out_specs=[pl.BlockSpec(shape.shape, whole3)] * 2,
            scratch_shapes=[pltpu.VMEM((4, slots * tokens + BLOCK, features), BF16)],
        ),
        out_shape=[shape, shape],
        compiler_params=pltpu.CompilerParams(vmem_limit_bytes=60 * 1024 * 1024),
        cost_estimate=pl.CostEstimate(
            flops=8 * slots * tokens * features * hidden,
            bytes_accessed=30_000_000,
            transcendentals=0,
        ),
    )(starts, picks, tiles, source, states, ranks, shares, *own, *other)


def body(policy_states, row_lengths, send_order, expert_ids, gate_codes, w_gate, w_up, w_down):
    features = policy_states.shape[3]
    maxlen = policy_states.shape[2]
    top = expert_ids.shape[-1]
    x, y, core = (lax.axis_index(name) for name in PLANE)
    column = (x * 4 + y) * 2 + core
    device = lax.axis_index("dp") * 32 + column
    swap = [(0, 1), (1, 0)]
    other = [lax.ppermute(w, "core", swap) for w in (w_gate, w_up, w_down)]

    packed = jnp.concatenate([row_lengths, send_order])
    spread = lax.all_to_all(
        jnp.broadcast_to(packed[None], (32, 16)), PLANE, 0, 0, tiled=True
    )
    lengths = spread[:, :8].T.reshape(256)
    held_by = (spread[:, 8:].T * 32 + jnp.arange(32, dtype=I32)[None, :]).reshape(256)
    every = jnp.arange(256, dtype=I32)
    offsets = jnp.sum(jnp.where(every[None, :] < every[:, None], lengths[None, :], 0), axis=1)
    is_holder = held_by[:, None] == every[None, :]
    judge_offsets = jnp.sum(jnp.where(is_holder, offsets[None, :], 0), axis=1)
    judge_lengths = jnp.sum(jnp.where(is_holder, lengths[None, :], 0), axis=1)
    at_me = every == device
    mine = jnp.sum(jnp.where(at_me, offsets, 0))
    judged_at = jnp.sum(jnp.where(at_me, judge_offsets, 0))
    judged_len = jnp.sum(jnp.where(at_me, judge_lengths, 0))

    pairs = jnp.arange(2 * 256, dtype=I32)
    peer, turn = pairs // 2, pairs % 2
    positions = jnp.arange(maxlen, dtype=I32)
    sent = lambda offset: (peer - offset) % 256 + 256 * turn
    rows = pick(one_hot(sent(mine), positions), policy_states.reshape(maxlen, features))
    names = jnp.concatenate(
        [
            expert_ids.reshape(maxlen, top).astype(BF16),
            gate_codes.reshape(maxlen, top).astype(BF16),
            jnp.zeros((maxlen, 128 - 2 * top), BF16),
        ],
        axis=1,
    )
    names = pick(one_hot(sent(judged_at), positions), names)
    outbound = jnp.concatenate([rows, names], axis=1).reshape(256, 2, features + 128)
    inbound = lax.all_to_all(outbound, ALL, 0, 0, tiled=True).reshape(512, features + 128)

    def slots_of(offset, length):
        offset, length = jnp.repeat(offset, 2), jnp.repeat(length, 2)
        position = (device - offset) % 256 + 256 * turn
        return jnp.where(position < length, (offset + position) // 256, -1)

    to_slot = one_hot(every, slots_of(offsets, lengths))
    judge_slot = one_hot(every, slots_of(judge_offsets, judge_lengths))
    states = pick(to_slot, inbound[:, :features])
    named = lax.dot_general(
        inbound[:, features : features + 16], judge_slot, (((0,), (1,)), ((), ())),
        preferred_element_type=F32,
    ).astype(BF16)

    all_named = lax.all_gather(named, ("x", "y"), axis=0).reshape(4, 4, 16, 256)
    all_named = lax.dynamic_slice_in_dim(jnp.concatenate([all_named, all_named], 0), x, 4, 0)
    all_named = lax.dynamic_slice_in_dim(jnp.concatenate([all_named, all_named], 1), y, 4, 1)
    near = jnp.arange(16, dtype=I32)
    source = (x + near // 4) % 4 * 4 + (y + near % 4) % 4
    experts = jnp.stack([2 * column, 2 * column + 1, 2 * (column ^ 1), 2 * (column ^ 1) + 1])
    below = (jnp.arange(BLOCK)[:, None] < jnp.arange(BLOCK)[None, :]).astype(BF16)
    size = 256 // CHUNKS
    blocks = 16 * size // BLOCK
    finished = []
    for chunk in range(CHUNKS):
        gathered = lax.all_gather(
            states[chunk * size : (chunk + 1) * size], ("x", "y"), axis=0
        )
        named_here = all_named[..., chunk * size : (chunk + 1) * size]
        named_here = named_here.transpose(2, 0, 1, 3).reshape(16, 16 * size)
        codes = named_here[top : 2 * top].astype(F32)
        share = codes / jnp.sum(codes, axis=0, keepdims=True)
        hit = named_here[None, :top].astype(I32) == experts[:, None, None]
        mask = jnp.any(hit, axis=1)
        shares = jnp.sum(jnp.where(hit, share[None], 0.0), axis=1)
        mask = mask.reshape(4, blocks, BLOCK)
        rank = jnp.dot(
            mask.reshape(4 * blocks, BLOCK).astype(BF16), below, preferred_element_type=F32
        ).reshape(4, blocks, BLOCK)
        ranks = jnp.where(mask, rank, -1.0).transpose(1, 0, 2)
        shares = shares.reshape(4, blocks, BLOCK).transpose(1, 0, 2)
        count = jnp.sum(mask.astype(I32), axis=2)
        taken = (count + 15) // 16 * 16
        earlier = jnp.arange(blocks)[None, :] < jnp.arange(blocks)[:, None]
        starts = jnp.sum(jnp.where(earlier[None], taken[:, None, :], 0), axis=2)
        tiles = (jnp.sum(taken, axis=1) + BLOCK - 1) // BLOCK
        picks = jnp.max((count + PICK - 1) // PICK, axis=0)
        out_a, out_b = run_experts(
            starts.reshape(-1), picks, tiles, source, gathered, ranks, shares,
            (w_gate, w_up, w_down), other,
        )
        flat = 8 * size
        finished.append(ring_sum(ring_sum(out_a.reshape(flat, features), "y"), "x"))
        finished.append(ring_sum(ring_sum(out_b.reshape(flat, features), "x"), "y"))

    made = jnp.concatenate(finished)
    back = lax.dot_general(
        judge_slot, made, (((0,), (0,)), ((), ())), preferred_element_type=F32
    ).astype(BF16)
    back = lax.all_to_all(back.reshape(256, 2, features), ALL, 0, 0, tiled=True)
    found = jnp.where(
        positions < judged_len, (positions + judged_at) % 256 * 2 + positions // 256, -1
    )
    result = pick(one_hot(found, pairs), back.reshape(512, features))
    return result.reshape(1, maxlen, features)


def solution(mesh):
    fine = Mesh(mesh.devices.reshape(8, 4, 4, 2), ALL)
    in_specs = (
        P(PLANE, "dp", None, None),
        P(PLANE),
        P(PLANE),
        P("dp", PLANE, None, None),
        P("dp", PLANE, None, None),
        P(PLANE, None, None),
        P(PLANE, None, None),
        P(PLANE, None, None),
    )
    return jax.shard_map(
        body, mesh=fine, in_specs=in_specs, out_specs=P(ALL, None, None), check_vma=False
    )
```

time: 572 us -> 345 us (0.60)
  the two profiles are of different devices: /device:TPU:12 before, /device:TPU:1 now
where the time goes in v1:
time: 345 us; the launch traced here: 338 us
  waiting for transfers between devices  120 us (35%)
  starting transfers between devices  77.7 us (23%)
  Pallas kernels  50.2 us (15%)
  local copies, waits for them, and re-layouts  33.7 us (10%)
  blocking collectives  18.1 us (5%)
  other arithmetic  16.4 us (5%)
  between operations  14.5 us (4%)
  matrix products  7.83 us (2%)
    pallas_call x2, Pallas kernels, run_experts(): pl.pallas_call(expert_kernel, grid_spec=pltpu.PrefetchScalarGridSpec(num_...  50.2 us
    ppermute x32, starting transfers between devices, shift(): lax.ppermute(value, axis, [(i, (i + by) % size) for i in range(size)])  40.9 us
    all_to_all x1, waiting for transfers between devices, body(): lax.all_to_all(outbound, ALL, 0, 0, tiled=True).reshape(512, features + 128)  32.7 us
    all_gather x2, waiting for transfers between devices, body(): lax.all_gather(states[chunk * size:(chunk + 1) * size], ('x', 'y'), axis=0)  30.1 us
    all_to_all x1, waiting for transfers between devices, body(): back = lax.all_to_all(back.reshape(256, 2, features), ALL, 0, 0, tiled=True)  28.5 us
    ppermute x32, waiting for transfers between devices, shift(): lax.ppermute(value, axis, [(i, (i + by) % size) for i in range(size)])  22.8 us
    all_gather x1, blocking collectives, body(): all_named = lax.all_gather(named, ('x', 'y'), axis=0).reshape(4, 4, 16, 256)  18.1 us
    all_to_all x1, starting transfers between devices, body(): back = lax.all_to_all(back.reshape(256, 2, features), ALL, 0, 0, tiled=True)  15.2 us
  transfers between devices with their start and end apart: 40, of which 13 were waited for; matrix products, arithmetic and copies ran while one was open for 13% of the time, Pallas kernels for 15%

profile of v1, /device:TPU:1, one launch (start us, length us, event | category | flops | bytes accessed | tf_op | source)
XLA Modules:
  0.0 338.2 jit_solution(10863513119030830472)
XLA Ops:
  8.0 8.6 %all-to-all-start = ((s32[32,1,16]{2,1,0:T(1,128)}), s32[32,1,16]{2,1,0:T(1,128)S(1)}, u32[]{:S(2)}, u32[]{:S(2)}) async-start(s32[32,1,16]{2,1,0:T(1,128)} %broadcast_in_dim.142), calls=%async_computation | async-start | bytes 32768 | tf_op jit(solution)/shard_map/all_to_all | solution.py:183
  18.5 4.9 %all-to-all-done = s32[32,1,16]{2,1,0:T(1,128)S(1)} async-done(((s32[32,1,16]{2,1,0:T(1,128)}), s32[32,1,16]{2,1,0:T(1,128)S(1)}, u32[]{:S(2)}, u32[]{:S(2)}) %all-to-all-start) | async-done | bytes 2080 | tf_op jit(solution)/shard_map/all_to_all | solution.py:183
  27.4 1.3 reshape.452
  28.8 11.0 %all-to-all-start.1 = ((bf16[256,2,1152]{2,1,0:T(2,128)(2,1)}), bf16[256,2,1152]{2,1,0:T(2,128)(2,1)S(1)}, u32[]{:S(2)}, u32[]{:S(2)}) async-start(bf16[256,2,1152]{2,1,0:T(2,128)(2,1)} %reshape.452), calls=%async_computation.1 | async-start | bytes 2359296 | tf_op jit(solution)/shard_map/all_to_all | solution.py:213
  40.3 32.7 %all-to-all-done.1 = bf16[256,2,1152]{2,1,0:T(2,128)(2,1)S(1)} async-done(((bf16[256,2,1152]{2,1,0:T(2,128)(2,1)}), bf16[256,2,1152]{2,1,0:T(2,128)(2,1)S(1)}, u32[]{:S(2)}, u32[]{:S(2)}) %all-to-all-start.1) | async-done | bytes 1179680 | tf_op jit(solution)/shard_map/all_to_all | solution.py:213
  73.0 1.3 reshape.453
  74.3 1.8 convolution_convert_fusion.3
  77.8 1.5 collective-permute-start
  79.8 2.8 copy.62.gate0
  82.6 4.7 %copy.63.up0 = bf16[2,1024,704]{2,1,0:T(8,128)(2,1)} copy(bf16[2,1024,704]{1,2,0:T(8,128)(2,1)} %param.14) | data formatting | bytes 5767168 | tf_op args[6]
  88.5 1.1 convolution_convert_fusion.5
  89.6 18.1 %all-gather = bf16[256,256]{1,0:T(8,128)(2,1)S(1)} all-gather(bf16[16,256]{1,0:T(8,128)(2,1)S(1)} %convolution_convert_fusion.5), channel_id=2, replica_groups=mesh['dp'=8,'x'=4,'y'=4,'core'=2] {'x','y'}, dimensions={0}, use_global_device_ids=true | all-gather | bytes 139264 | tf_op jit(solution)/shard_map/all_gather | solution.py:228
  115.1 4.6 %copy.64.gate1 = bf16[2,1024,704]{2,1,0:T(8,128)(2,1)} copy(bf16[2,1024,704]{1,2,0:T(8,128)(2,1)} %collective-permute-done) | data formatting | bytes 5767168 | tf_op jit(solution)/shard_map/ppermute | solution.py:180
  119.8 4.6 %copy.65.up1 = bf16[2,1024,704]{2,1,0:T(8,128)(2,1)} copy(bf16[2,1024,704]{1,2,0:T(8,128)(2,1)} %collective-permute-done.1) | data formatting | bytes 5767168 | tf_op jit(solution)/shard_map/ppermute | solution.py:180
  124.4 4.3 %all-gather.6.cloned.1.call-done = bf16[2048,1024]{1,0:T(8,128)(2,1)} async-done(((bf16[128,1024]{1,0:T(8,128)(2,1)}), bf16[2048,1024]{1,0:T(8,128)(2,1)}) %all-gather.6.cloned.1.call-update) | async-done | bytes 4194320 | tf_op jit(solution)/shard_map/all_gather | solution.py:239
  128.7 25.1 %shard_map.82 = (bf16[16,64,1024]{2,1,0:T(8,128)(2,1)}, bf16[16,64,1024]{2,1,0:T(8,128)(2,1)}) custom-call(s32[32]{0:T(128)} %reshape.456.starts, s32[8]{0:T(128)} %get-tuple-element.81.picks, s32[4]{0:T(128)} %and_select_fusion.5.tiles, s32[16]{0:T(128)} %fusion.90.source, bf16[16,128,1024]{2,1,0:T(8,128)(2,1)} %bitcast.136, f32[8,4,256]{2,1,0:T(4,128)} %fusion.1.ranks, ...), custom_call_target="tpu_custom_call" | custom-call | flops 11811160064 | bytes 30000000 | tf_op jit(solution)/shard_map/pallas_call | solution.py:147
  153.8 2.6 fusion.101
  156.4 4.2 %collective-permute-start.3 = (bf16[128,1024]{1,0:T(8,128)(2,1)}, bf16[128,1024]{1,0:T(8,128)(2,1)}, u32[]{:S(2)}, u32[]{:S(2)}) collective-permute-start(bf16[128,1024]{1,0:T(8,128)(2,1)} %bitcast.23), channel_id=1, source_target_pairs={{0,6},{2,0},{4,2},{6,4},{1,7},{3,1},{5,3},{7,5},{8,14},{10,8},{12,... | collective-permute-start | bytes 786440 | tf_op jit(solution)/shard_map/ppermute | solution.py:30
  161.5 25.8 %all-gather.8.cloned.1.call-done = bf16[2048,1024]{1,0:T(8,128)(2,1)} async-done(((bf16[128,1024]{1,0:T(8,128)(2,1)}), bf16[2048,1024]{1,0:T(8,128)(2,1)}) %all-gather.8.cloned.1.call-update) | async-done | bytes 4194320 | tf_op jit(solution)/shard_map/all_gather | solution.py:239
  187.3 25.0 %shard_map.83 = (bf16[16,64,1024]{2,1,0:T(8,128)(2,1)}, bf16[16,64,1024]{2,1,0:T(8,128)(2,1)}) custom-call(s32[32]{0:T(128)} %reshape.461.starts, s32[8]{0:T(128)} %get-tuple-element.82.picks, s32[4]{0:T(128)} %and_select_fusion.tiles, s32[16]{0:T(128)} %fusion.90.source, bf16[16,128,1024]{2,1,0:T(8,128)(2,1)} %bitcast.135, f32[8,4,256]{2,1,0:T(4,128)} %fusion.2.ranks, ...), custom_call_target="tpu_custom_call" | custom-call | flops 11811160064 | bytes 30000000 | tf_op jit(solution)/shard_map/pallas_call | solution.py:147
  212.3 1.6 fusion.103
  214.6 1.1 slice.360
  215.7 1.1 slice.400
  216.9 4.5 %collective-permute-start.11 = (bf16[128,1024]{1,0:T(8,128)(2,1)S(1)}, bf16[128,1024]{1,0:T(8,128)(2,1)S(1)}, u32[]{:S(2)}, u32[]{:S(2)}) collective-permute-start(bf16[128,1024]{1,0:T(8,128)(2,1)S(1)} %bitcast.118), channel_id=1, source_target_pairs={{0,24},{8,0},{16,8},{24,16},{1,25},{9,1},{17,9},{25,17},{2,26},{10... | collective-permute-start | bytes 786440 | tf_op jit(solution)/shard_map/ppermute | solution.py:30
  221.7 2.1 collective-permute-start.19
  224.8 2.1 collective-permute-start.27
  228.3 2.9 collective-permute-done.13
  231.2 1.3 collective-permute-start.4
  235.4 2.9 collective-permute-start.20
  238.4 5.9 %collective-permute-done.4 = bf16[256,1024]{1,0:T(8,128)(2,1)S(1)} collective-permute-done((bf16[256,1024]{1,0:T(8,128)(2,1)S(1)}, bf16[256,1024]{1,0:T(8,128)(2,1)S(1)}, u32[]{:S(2)}, u32[]{:S(2)}) %collective-permute-start.4) | collective-permute-done | bytes 524320 | tf_op jit(solution)/shard_map/ppermute | solution.py:30
  244.3 2.4 collective-permute-done.6
  247.0 1.5 collective-permute-start.30
  248.5 1.2 collective-permute-start.7
  250.1 5.4 %collective-permute-done.20 = bf16[256,1024]{1,0:T(8,128)(2,1)S(1)} collective-permute-done((bf16[256,1024]{1,0:T(8,128)(2,1)S(1)}, bf16[256,1024]{1,0:T(8,128)(2,1)S(1)}, u32[]{:S(2)}, u32[]{:S(2)}) %collective-permute-start.20) | collective-permute-done | bytes 524320 | tf_op jit(solution)/shard_map/ppermute | solution.py:30
  256.8 1.7 collective-permute-start.15
  258.9 2.7 collective-permute-start.23
  262.0 2.7 collective-permute-start.31
  264.9 2.7 collective-permute-start.8
  267.7 2.7 collective-permute-start.16
  270.6 2.7 collective-permute-start.24
  273.4 2.7 collective-permute-start.32
  276.5 2.2 collective-permute-done.26
  278.8 2.6 collective-permute-done.34
  282.0 1.2 reshape.463
  283.2 15.2 %all-to-all-start.2 = ((bf16[256,2,1024]{2,1,0:T(2,128)(2,1)}), bf16[256,2,1024]{2,1,0:T(2,128)(2,1)S(1)}, u32[]{:S(2)}, u32[]{:S(2)}) async-start(bf16[256,2,1024]{2,1,0:T(2,128)(2,1)} %reshape.463), calls=%async_computation.2 | async-start | bytes 2097152 | tf_op jit(solution)/shard_map/all_to_all | solution.py:273
  299.1 1.3 fusion.66
  300.4 28.5 %all-to-all-done.2 = bf16[256,2,1024]{2,1,0:T(2,128)(2,1)S(1)} async-done(((bf16[256,2,1024]{2,1,0:T(2,128)(2,1)}), bf16[256,2,1024]{2,1,0:T(2,128)(2,1)S(1)}, u32[]{:S(2)}, u32[]{:S(2)}) %all-to-all-start.2) | async-done | bytes 1048608 | tf_op jit(solution)/shard_map/all_to_all | solution.py:273
  329.4 1.7 fusion
  (181 shorter events, 30.8 us)
Async XLA Ops:
  6.5 19.6 %copy-start = (bf16[1,1,512,1024]{3,2,1,0:T(8,128)(2,1)S(1)}, bf16[1,1,512,1024]{3,2,1,0:T(8,128)(2,1)}, u32[]{:S(2)}) copy-start(bf16[1,1,512,1024]{3,2,1,0:T(8,128)(2,1)} %param.8) | copy-start | bytes 3145732
  8.0 15.5 %all-to-all-start = ((s32[32,1,16]{2,1,0:T(1,128)}), s32[32,1,16]{2,1,0:T(1,128)S(1)}, u32[]{:S(2)}, u32[]{:S(2)}) async-start(s32[32,1,16]{2,1,0:T(1,128)} %broadcast_in_dim.142), calls=%async_computation | async-start | bytes 32768 | tf_op jit(solution)/shard_map/all_to_all | solution.py:183
  28.8 44.3 %all-to-all-start.1 = ((bf16[256,2,1152]{2,1,0:T(2,128)(2,1)}), bf16[256,2,1152]{2,1,0:T(2,128)(2,1)S(1)}, u32[]{:S(2)}, u32[]{:S(2)}) async-start(bf16[256,2,1152]{2,1,0:T(2,128)(2,1)} %reshape.452), calls=%async_computation.1 | async-start | bytes 2359296 | tf_op jit(solution)/shard_map/all_to_all | solution.py:213
  39.7 88.9 %all-gather.6.cloned.1.call-start = ((), (), s32[]{:S(2)}) async-start(), calls=%async_computation.3 | async-start | bytes 4456448 | tf_op jit(solution)/shard_map/all_gather | solution.py:239
  74.3 3.4 %copy-start.2 = (bf16[2,1024,704]{1,2,0:T(8,128)(2,1)S(1)}, bf16[2,1024,704]{1,2,0:T(8,128)(2,1)}, u32[]{:S(2)}) copy-start(bf16[2,1024,704]{1,2,0:T(8,128)(2,1)} %param.13) | copy-start | bytes 8650756
  77.0 110.3 %all-gather.8.cloned.1.call-start = ((), (), s32[]{:S(2)}) async-start(), calls=%async_computation.4 | async-start | bytes 4456448 | tf_op jit(solution)/shard_map/all_gather | solution.py:239
  77.8 37.4 %collective-permute-start = (bf16[2,1024,704]{1,2,0:T(8,128)(2,1)S(1)}, bf16[2,1024,704]{1,2,0:T(8,128)(2,1)}, u32[]{:S(2)}, u32[]{:S(2)}) collective-permute-start(bf16[2,1024,704]{1,2,0:T(8,128)(2,1)S(1)} %copy-done.2), channel_id=1, source_target_pairs={{0,1},{1,0},{2,3},{3,2},{4,5},{5,4},{6,7},{7,6},{8,9},{9,8},{10,11... | collective-permute-start | bytes 8650760 | tf_op jit(solution)/shard_map/ppermute | solution.py:180
  79.3 40.5 %collective-permute-start.1 = (bf16[2,1024,704]{1,2,0:T(8,128)(2,1)}, bf16[2,1024,704]{1,2,0:T(8,128)(2,1)}, u32[]{:S(2)}, u32[]{:S(2)}) collective-permute-start(bf16[2,1024,704]{1,2,0:T(8,128)(2,1)} %param.14), channel_id=1, source_target_pairs={{0,1},{1,0},{2,3},{3,2},{4,5},{5,4},{6,7},{7,6},{8,9},{9,8},{10,11... | collective-permute-start | bytes 8650760 | tf_op jit(solution)/shard_map/ppermute | solution.py:180
  79.4 45.0 %collective-permute-start.2 = (bf16[2,704,1024]{2,1,0:T(8,128)(2,1)}, bf16[2,704,1024]{2,1,0:T(8,128)(2,1)}, u32[]{:S(2)}, u32[]{:S(2)}) collective-permute-start(bf16[2,704,1024]{2,1,0:T(8,128)(2,1)} %down0.3), channel_id=1, source_target_pairs={{0,1},{1,0},{2,3},{3,2},{4,5},{5,4},{6,7},{7,6},{8,9},{9,8},{10,11... | collective-permute-start | bytes 8650760 | tf_op jit(solution)/shard_map/ppermute | solution.py:180
  153.8 6.8 %copy-start.3 = (bf16[16,64,1024]{2,1,0:T(8,128)(2,1)S(1)}, bf16[16,64,1024]{2,1,0:T(8,128)(2,1)}, u32[]{:S(2)}) copy-start(bf16[16,64,1024]{2,1,0:T(8,128)(2,1)} %get-tuple-element.10) | copy-start | bytes 6291460
  156.4 67.4 %collective-permute-start.3 = (bf16[128,1024]{1,0:T(8,128)(2,1)}, bf16[128,1024]{1,0:T(8,128)(2,1)}, u32[]{:S(2)}, u32[]{:S(2)}) collective-permute-start(bf16[128,1024]{1,0:T(8,128)(2,1)} %bitcast.23), channel_id=1, source_target_pairs={{0,6},{2,0},{4,2},{6,4},{1,7},{3,1},{5,3},{7,5},{8,14},{10,8},{12,... | collective-permute-start | bytes 786440 | tf_op jit(solution)/shard_map/ppermute | solution.py:30
  160.6 64.2 %collective-permute-start.5 = (bf16[128,1024]{1,0:T(8,128)(2,1)}, bf16[128,1024]{1,0:T(8,128)(2,1)}, u32[]{:S(2)}, u32[]{:S(2)}) collective-permute-start(bf16[128,1024]{1,0:T(8,128)(2,1)} %bitcast.27), channel_id=1, source_target_pairs={{0,2},{2,4},{4,6},{6,0},{1,3},{3,5},{5,7},{7,1},{8,10},{10,12},{12... | collective-permute-start | bytes 786440 | tf_op jit(solution)/shard_map/ppermute | solution.py:30
  214.5 6.9 %copy-start.8 = (bf16[2,64,1024]{2,1,0:T(8,128)(2,1)S(1)}, bf16[2,64,1024]{2,1,0:T(8,128)(2,1)}, u32[]{:S(2)}) copy-start(bf16[2,64,1024]{2,1,0:T(8,128)(2,1)} %get-tuple-element.32) | copy-start | bytes 786436
  215.7 12.4 %copy-start.7 = (bf16[2,64,1024]{2,1,0:T(8,128)(2,1)S(1)}, bf16[2,64,1024]{2,1,0:T(8,128)(2,1)}, u32[]{:S(2)}) copy-start(bf16[2,64,1024]{2,1,0:T(8,128)(2,1)} %get-tuple-element.29) | copy-start | bytes 786436
  216.9 11.3 %copy-start.6 = (bf16[2,64,1024]{2,1,0:T(8,128)(2,1)S(1)}, bf16[2,64,1024]{2,1,0:T(8,128)(2,1)}, u32[]{:S(2)}) copy-start(bf16[2,64,1024]{2,1,0:T(8,128)(2,1)} %get-tuple-element.28) | copy-start | bytes 786436
  216.9 11.0 %collective-permute-start.11 = (bf16[128,1024]{1,0:T(8,128)(2,1)S(1)}, bf16[128,1024]{1,0:T(8,128)(2,1)S(1)}, u32[]{:S(2)}, u32[]{:S(2)}) collective-permute-start(bf16[128,1024]{1,0:T(8,128)(2,1)S(1)} %bitcast.118), channel_id=1, source_target_pairs={{0,24},{8,0},{16,8},{24,16},{1,25},{9,1},{17,9},{25,17},{2,26},{10... | collective-permute-start | bytes 786440 | tf_op jit(solution)/shard_map/ppermute | solution.py:30
  221.5 9.7 %collective-permute-start.13 = (bf16[128,1024]{1,0:T(8,128)(2,1)S(1)}, bf16[128,1024]{1,0:T(8,128)(2,1)S(1)}, u32[]{:S(2)}, u32[]{:S(2)}) collective-permute-start(bf16[128,1024]{1,0:T(8,128)(2,1)S(1)} %bitcast.116), channel_id=1, source_target_pairs={{0,8},{8,16},{16,24},{24,0},{1,9},{9,17},{17,25},{25,1},{2,10},{10... | collective-permute-start | bytes 786440 | tf_op jit(solution)/shard_map/ppermute | solution.py:30
  221.7 10.9 %collective-permute-start.19 = (bf16[128,1024]{1,0:T(8,128)(2,1)S(1)}, bf16[128,1024]{1,0:T(8,128)(2,1)S(1)}, u32[]{:S(2)}, u32[]{:S(2)}) collective-permute-start(bf16[128,1024]{1,0:T(8,128)(2,1)S(1)} %bitcast.117), channel_id=1, source_target_pairs={{0,6},{2,0},{4,2},{6,4},{1,7},{3,1},{5,3},{7,5},{8,14},{10,8},{12,... | collective-permute-start | bytes 786440 | tf_op jit(solution)/shard_map/ppermute | solution.py:30
  223.8 9.2 %collective-permute-start.21 = (bf16[128,1024]{1,0:T(8,128)(2,1)S(1)}, bf16[128,1024]{1,0:T(8,128)(2,1)S(1)}, u32[]{:S(2)}, u32[]{:S(2)}) collective-permute-start(bf16[128,1024]{1,0:T(8,128)(2,1)S(1)} %bitcast.115), channel_id=1, source_target_pairs={{0,2},{2,4},{4,6},{6,0},{1,3},{3,5},{5,7},{7,1},{8,10},{10,12},{12... | collective-permute-start | bytes 786440 | tf_op jit(solution)/shard_map/ppermute | solution.py:30
  224.8 9.3 %collective-permute-start.27 = (bf16[128,1024]{1,0:T(8,128)(2,1)S(1)}, bf16[128,1024]{1,0:T(8,128)(2,1)S(1)}, u32[]{:S(2)}, u32[]{:S(2)}) collective-permute-start(bf16[128,1024]{1,0:T(8,128)(2,1)S(1)} %bitcast.114), channel_id=1, source_target_pairs={{0,24},{8,0},{16,8},{24,16},{1,25},{9,1},{17,9},{25,17},{2,26},{10... | collective-permute-start | bytes 786440 | tf_op jit(solution)/shard_map/ppermute | solution.py:30
  228.0 7.4 %collective-permute-start.29 = (bf16[128,1024]{1,0:T(8,128)(2,1)S(1)}, bf16[128,1024]{1,0:T(8,128)(2,1)S(1)}, u32[]{:S(2)}, u32[]{:S(2)}) collective-permute-start(bf16[128,1024]{1,0:T(8,128)(2,1)S(1)} %bitcast.113), channel_id=1, source_target_pairs={{0,8},{8,16},{16,24},{24,0},{1,9},{9,17},{17,25},{25,1},{2,10},{10... | collective-permute-start | bytes 786440 | tf_op jit(solution)/shard_map/ppermute | solution.py:30
  228.0 4.9 %copy-start.5 = (bf16[2,64,1024]{2,1,0:T(8,128)(2,1)S(1)}, bf16[2,64,1024]{2,1,0:T(8,128)(2,1)}, u32[]{:S(2)}) copy-start(bf16[2,64,1024]{2,1,0:T(8,128)(2,1)} %get-tuple-element.35) | copy-start | bytes 786436
  231.2 13.1 %collective-permute-start.4 = (bf16[256,1024]{1,0:T(8,128)(2,1)S(1)}, bf16[256,1024]{1,0:T(8,128)(2,1)S(1)}, u32[]{:S(2)}, u32[]{:S(2)}) collective-permute-start(bf16[256,1024]{1,0:T(8,128)(2,1)S(1)} %pad_maximum_fusion.1), channel_id=1, source_target_pairs={{0,6},{2,0},{4,2},{6,4},{1,7},{3,1},{5,3},{7,5},{8,14},{10,8},{12,... | collective-permute-start | bytes 1572872 | tf_op jit(solution)/shard_map/ppermute | solution.py:30
  232.6 14.0 %collective-permute-start.6 = (bf16[256,1024]{1,0:T(8,128)(2,1)S(1)}, bf16[256,1024]{1,0:T(8,128)(2,1)S(1)}, u32[]{:S(2)}, u32[]{:S(2)}) collective-permute-start(bf16[256,1024]{1,0:T(8,128)(2,1)S(1)} %pad_maximum_fusion.2), channel_id=1, source_target_pairs={{0,2},{2,4},{4,6},{6,0},{1,3},{3,5},{5,7},{7,1},{8,10},{10,12},{12... | collective-permute-start | bytes 1572872 | tf_op jit(solution)/shard_map/ppermute | solution.py:30
  233.0 14.0 %collective-permute-start.12 = (bf16[256,1024]{1,0:T(8,128)(2,1)S(1)}, bf16[256,1024]{1,0:T(8,128)(2,1)S(1)}, u32[]{:S(2)}, u32[]{:S(2)}) collective-permute-start(bf16[256,1024]{1,0:T(8,128)(2,1)S(1)} %pad_maximum_fusion.3), channel_id=1, source_target_pairs={{0,24},{8,0},{16,8},{24,16},{1,25},{9,1},{17,9},{25,17},{2,26},{10... | collective-permute-start | bytes 1572872 | tf_op jit(solution)/shard_map/ppermute | solution.py:30
  234.1 14.4 %collective-permute-start.14 = (bf16[256,1024]{1,0:T(8,128)(2,1)S(1)}, bf16[256,1024]{1,0:T(8,128)(2,1)S(1)}, u32[]{:S(2)}, u32[]{:S(2)}) collective-permute-start(bf16[256,1024]{1,0:T(8,128)(2,1)S(1)} %pad_maximum_fusion.4), channel_id=1, source_target_pairs={{0,8},{8,16},{16,24},{24,0},{1,9},{9,17},{17,25},{25,1},{2,10},{10... | collective-permute-start | bytes 1572872 | tf_op jit(solution)/shard_map/ppermute | solution.py:30
  235.4 20.1 %collective-permute-start.20 = (bf16[256,1024]{1,0:T(8,128)(2,1)S(1)}, bf16[256,1024]{1,0:T(8,128)(2,1)S(1)}, u32[]{:S(2)}, u32[]{:S(2)}) collective-permute-start(bf16[256,1024]{1,0:T(8,128)(2,1)S(1)} %pad_maximum_fusion.5), channel_id=1, source_target_pairs={{0,6},{2,0},{4,2},{6,4},{1,7},{3,1},{5,3},{7,5},{8,14},{10,8},{12,... | collective-permute-start | bytes 1572872 | tf_op jit(solution)/shard_map/ppermute | solution.py:30
  244.3 12.5 %collective-permute-start.22 = (bf16[256,1024]{1,0:T(8,128)(2,1)S(1)}, bf16[256,1024]{1,0:T(8,128)(2,1)S(1)}, u32[]{:S(2)}, u32[]{:S(2)}) collective-permute-start(bf16[256,1024]{1,0:T(8,128)(2,1)S(1)} %pad_maximum_fusion.6), channel_id=1, source_target_pairs={{0,2},{2,4},{4,6},{6,0},{1,3},{3,5},{5,7},{7,1},{8,10},{10,12},{12... | collective-permute-start | bytes 1572872 | tf_op jit(solution)/shard_map/ppermute | solution.py:30
  246.6 12.2 %collective-permute-start.28 = (bf16[256,1024]{1,0:T(8,128)(2,1)S(1)}, bf16[256,1024]{1,0:T(8,128)(2,1)S(1)}, u32[]{:S(2)}, u32[]{:S(2)}) collective-permute-start(bf16[256,1024]{1,0:T(8,128)(2,1)S(1)} %pad_maximum_fusion.7), channel_id=1, source_target_pairs={{0,24},{8,0},{16,8},{24,16},{1,25},{9,1},{17,9},{25,17},{2,26},{10... | collective-permute-start | bytes 1572872 | tf_op jit(solution)/shard_map/ppermute | solution.py:30
  247.0 12.0 %collective-permute-start.30 = (bf16[256,1024]{1,0:T(8,128)(2,1)S(1)}, bf16[256,1024]{1,0:T(8,128)(2,1)S(1)}, u32[]{:S(2)}, u32[]{:S(2)}) collective-permute-start(bf16[256,1024]{1,0:T(8,128)(2,1)S(1)} %pad_maximum_fusion.8), channel_id=1, source_target_pairs={{0,8},{8,16},{16,24},{24,0},{1,9},{9,17},{17,25},{25,1},{2,10},{10... | collective-permute-start | bytes 1572872 | tf_op jit(solution)/shard_map/ppermute | solution.py:30
  248.5 13.4 %collective-permute-start.7 = (bf16[32,1024]{1,0:T(8,128)(2,1)S(1)}, bf16[32,1024]{1,0:T(8,128)(2,1)S(1)}, u32[]{:S(2)}, u32[]{:S(2)}) collective-permute-start(bf16[32,1024]{1,0:T(8,128)(2,1)S(1)} %get-tuple-element.51), channel_id=1, source_target_pairs={{0,24},{8,0},{16,8},{24,16},{1,25},{9,1},{17,9},{25,17},{2,26},{10... | collective-permute-start | bytes 196616 | tf_op jit(solution)/shard_map/ppermute | solution.py:30
  255.5 6.5 %collective-permute-start.9 = (bf16[32,1024]{1,0:T(8,128)(2,1)S(1)}, bf16[32,1024]{1,0:T(8,128)(2,1)S(1)}, u32[]{:S(2)}, u32[]{:S(2)}) collective-permute-start(bf16[32,1024]{1,0:T(8,128)(2,1)S(1)} %get-tuple-element.52), channel_id=1, source_target_pairs={{0,8},{8,16},{16,24},{24,0},{1,9},{9,17},{17,25},{25,1},{2,10},{10... | collective-permute-start | bytes 196616 | tf_op jit(solution)/shard_map/ppermute | solution.py:30
  256.8 8.0 %collective-permute-start.15 = (bf16[32,1024]{1,0:T(8,128)(2,1)S(1)}, bf16[32,1024]{1,0:T(8,128)(2,1)S(1)}, u32[]{:S(2)}, u32[]{:S(2)}) collective-permute-start(bf16[32,1024]{1,0:T(8,128)(2,1)S(1)} %get-tuple-element.57), channel_id=1, source_target_pairs={{0,6},{2,0},{4,2},{6,4},{1,7},{3,1},{5,3},{7,5},{8,14},{10,8},{12,... | collective-permute-start | bytes 196616 | tf_op jit(solution)/shard_map/ppermute | solution.py:30
  258.8 6.0 %collective-permute-start.17 = (bf16[32,1024]{1,0:T(8,128)(2,1)S(1)}, bf16[32,1024]{1,0:T(8,128)(2,1)S(1)}, u32[]{:S(2)}, u32[]{:S(2)}) collective-permute-start(bf16[32,1024]{1,0:T(8,128)(2,1)S(1)} %get-tuple-element.58), channel_id=1, source_target_pairs={{0,2},{2,4},{4,6},{6,0},{1,3},{3,5},{5,7},{7,1},{8,10},{10,12},{12... | collective-permute-start | bytes 196616 | tf_op jit(solution)/shard_map/ppermute | solution.py:30
  258.9 8.7 %collective-permute-start.23 = (bf16[32,1024]{1,0:T(8,128)(2,1)S(1)}, bf16[32,1024]{1,0:T(8,128)(2,1)S(1)}, u32[]{:S(2)}, u32[]{:S(2)}) collective-permute-start(bf16[32,1024]{1,0:T(8,128)(2,1)S(1)} %get-tuple-element.65), channel_id=1, source_target_pairs={{0,24},{8,0},{16,8},{24,16},{1,25},{9,1},{17,9},{25,17},{2,26},{10... | collective-permute-start | bytes 196616 | tf_op jit(solution)/shard_map/ppermute | solution.py:30
  261.9 5.8 %collective-permute-start.25 = (bf16[32,1024]{1,0:T(8,128)(2,1)S(1)}, bf16[32,1024]{1,0:T(8,128)(2,1)S(1)}, u32[]{:S(2)}, u32[]{:S(2)}) collective-permute-start(bf16[32,1024]{1,0:T(8,128)(2,1)S(1)} %get-tuple-element.66), channel_id=1, source_target_pairs={{0,8},{8,16},{16,24},{24,0},{1,9},{9,17},{17,25},{25,1},{2,10},{10... | collective-permute-start | bytes 196616 | tf_op jit(solution)/shard_map/ppermute | solution.py:30
  262.0 8.4 %collective-permute-start.31 = (bf16[32,1024]{1,0:T(8,128)(2,1)S(1)}, bf16[32,1024]{1,0:T(8,128)(2,1)S(1)}, u32[]{:S(2)}, u32[]{:S(2)}) collective-permute-start(bf16[32,1024]{1,0:T(8,128)(2,1)S(1)} %get-tuple-element.71), channel_id=1, source_target_pairs={{0,6},{2,0},{4,2},{6,4},{1,7},{3,1},{5,3},{7,5},{8,14},{10,8},{12,... | collective-permute-start | bytes 196616 | tf_op jit(solution)/shard_map/ppermute | solution.py:30
  264.8 5.8 %collective-permute-start.33 = (bf16[32,1024]{1,0:T(8,128)(2,1)S(1)}, bf16[32,1024]{1,0:T(8,128)(2,1)S(1)}, u32[]{:S(2)}, u32[]{:S(2)}) collective-permute-start(bf16[32,1024]{1,0:T(8,128)(2,1)S(1)} %get-tuple-element.72), channel_id=1, source_target_pairs={{0,2},{2,4},{4,6},{6,0},{1,3},{3,5},{5,7},{7,1},{8,10},{10,12},{12... | collective-permute-start | bytes 196616 | tf_op jit(solution)/shard_map/ppermute | solution.py:30
  264.9 8.4 %collective-permute-start.8 = (bf16[64,1024]{1,0:T(8,128)(2,1)S(1)}, bf16[64,1024]{1,0:T(8,128)(2,1)S(1)}, u32[]{:S(2)}, u32[]{:S(2)}) collective-permute-start(bf16[64,1024]{1,0:T(8,128)(2,1)S(1)} %pad_maximum_fusion.9), channel_id=1, source_target_pairs={{0,24},{8,0},{16,8},{24,16},{1,25},{9,1},{17,9},{25,17},{2,26},{10... | collective-permute-start | bytes 393224 | tf_op jit(solution)/shard_map/ppermute | solution.py:30
  267.6 5.8 %collective-permute-start.10 = (bf16[64,1024]{1,0:T(8,128)(2,1)S(1)}, bf16[64,1024]{1,0:T(8,128)(2,1)S(1)}, u32[]{:S(2)}, u32[]{:S(2)}) collective-permute-start(bf16[64,1024]{1,0:T(8,128)(2,1)S(1)} %pad_maximum_fusion.10), channel_id=1, source_target_pairs={{0,8},{8,16},{16,24},{24,0},{1,9},{9,17},{17,25},{25,1},{2,10},{10... | collective-permute-start | bytes 393224 | tf_op jit(solution)/shard_map/ppermute | solution.py:30
  267.7 8.4 %collective-permute-start.16 = (bf16[64,1024]{1,0:T(8,128)(2,1)S(1)}, bf16[64,1024]{1,0:T(8,128)(2,1)S(1)}, u32[]{:S(2)}, u32[]{:S(2)}) collective-permute-start(bf16[64,1024]{1,0:T(8,128)(2,1)S(1)} %pad_maximum_fusion.11), channel_id=1, source_target_pairs={{0,6},{2,0},{4,2},{6,4},{1,7},{3,1},{5,3},{7,5},{8,14},{10,8},{12,... | collective-permute-start | bytes 393224 | tf_op jit(solution)/shard_map/ppermute | solution.py:30
  270.5 5.9 %collective-permute-start.18 = (bf16[64,1024]{1,0:T(8,128)(2,1)S(1)}, bf16[64,1024]{1,0:T(8,128)(2,1)S(1)}, u32[]{:S(2)}, u32[]{:S(2)}) collective-permute-start(bf16[64,1024]{1,0:T(8,128)(2,1)S(1)} %pad_maximum_fusion.12), channel_id=1, source_target_pairs={{0,2},{2,4},{4,6},{6,0},{1,3},{3,5},{5,7},{7,1},{8,10},{10,12},{12... | collective-permute-start | bytes 393224 | tf_op jit(solution)/shard_map/ppermute | solution.py:30
  270.6 5.9 %collective-permute-start.24 = (bf16[64,1024]{1,0:T(8,128)(2,1)S(1)}, bf16[64,1024]{1,0:T(8,128)(2,1)S(1)}, u32[]{:S(2)}, u32[]{:S(2)}) collective-permute-start(bf16[64,1024]{1,0:T(8,128)(2,1)S(1)} %pad_maximum_fusion.13), channel_id=1, source_target_pairs={{0,24},{8,0},{16,8},{24,16},{1,25},{9,1},{17,9},{25,17},{2,26},{10... | collective-permute-start | bytes 393224 | tf_op jit(solution)/shard_map/ppermute | solution.py:30
  273.3 5.4 %collective-permute-start.26 = (bf16[64,1024]{1,0:T(8,128)(2,1)S(1)}, bf16[64,1024]{1,0:T(8,128)(2,1)S(1)}, u32[]{:S(2)}, u32[]{:S(2)}) collective-permute-start(bf16[64,1024]{1,0:T(8,128)(2,1)S(1)} %pad_maximum_fusion.14), channel_id=1, source_target_pairs={{0,8},{8,16},{16,24},{24,0},{1,9},{9,17},{17,25},{25,1},{2,10},{10... | collective-permute-start | bytes 393224 | tf_op jit(solution)/shard_map/ppermute | solution.py:30
  273.4 5.4 %collective-permute-start.32 = (bf16[64,1024]{1,0:T(8,128)(2,1)S(1)}, bf16[64,1024]{1,0:T(8,128)(2,1)S(1)}, u32[]{:S(2)}, u32[]{:S(2)}) collective-permute-start(bf16[64,1024]{1,0:T(8,128)(2,1)S(1)} %pad_maximum_fusion.15), channel_id=1, source_target_pairs={{0,6},{2,0},{4,2},{6,4},{1,7},{3,1},{5,3},{7,5},{8,14},{10,8},{12,... | collective-permute-start | bytes 393224 | tf_op jit(solution)/shard_map/ppermute | solution.py:30
  276.2 5.3 %collective-permute-start.34 = (bf16[64,1024]{1,0:T(8,128)(2,1)S(1)}, bf16[64,1024]{1,0:T(8,128)(2,1)S(1)}, u32[]{:S(2)}, u32[]{:S(2)}) collective-permute-start(bf16[64,1024]{1,0:T(8,128)(2,1)S(1)} %pad_maximum_fusion.16), channel_id=1, source_target_pairs={{0,2},{2,4},{4,6},{6,0},{1,3},{3,5},{5,7},{7,1},{8,10},{10,12},{12... | collective-permute-start | bytes 393224 | tf_op jit(solution)/shard_map/ppermute | solution.py:30
  283.2 45.8 %all-to-all-start.2 = ((bf16[256,2,1024]{2,1,0:T(2,128)(2,1)}), bf16[256,2,1024]{2,1,0:T(2,128)(2,1)S(1)}, u32[]{:S(2)}, u32[]{:S(2)}) async-start(bf16[256,2,1024]{2,1,0:T(2,128)(2,1)} %reshape.463), calls=%async_computation.2 | async-start | bytes 2097152 | tf_op jit(solution)/shard_map/all_to_all | solution.py:273
  299.1 32.0 %copy-start.1 = (bf16[1,1,512,1024]{3,2,1,0:T(8,128)(2,1)S(1)}, bf16[1,1,512,1024]{3,2,1,0:T(8,128)(2,1)}, u32[]{:S(2)}) copy-start(bf16[1,1,512,1024]{3,2,1,0:T(8,128)(2,1)} %param.8) | copy-start | bytes 3145732
  (2 other events, 4.4 us)
Sparse Core Ops, SparseCore 0:
  77.1 51.5 all-gather.5
  131.1 56.1 all-gather.7
